TPU v7x, 32 devices: a whole 2x2x4 slice. The times are simulated.
32 devices in a mesh: chan: 4 (over y, x), ctx: 8 (over z, core).
Axes of the slice: x: 2, y: 2, z: 4, core: 2. Of those that a mesh axis runs over, the one named last changes fastest.
Arguments:
- gate_stream: bfloat16 [2048, 4096], P('ctx', 'chan'), may hold values from -6 to 6
- key_stream: bfloat16 [2048, 4096], P('ctx', 'chan'), may hold values from -6 to 6
- value_stream: bfloat16 [2048, 4096], P('ctx', 'chan'), may hold values from -6 to 6
- residues: float32 [16, 4096], P(None, 'chan'), may hold values from -4 to 4
- decay_rates: float32 [16, 4096], P(None, 'chan'), may hold values from 9.765625e-06 to 0.05
- out_weight: bfloat16 [4096, 4096], P('chan'), may hold values from -0.125 to 0.125
Outputs:
- projected: bfloat16 [2048, 4096], P('ctx', 'chan')
All inputs are finite; a program needn't handle non-finite values.
Results may differ from a plain program's by a relative error of at most 0.006.
Values sent between devices are 32-bit elements; how exact they have to be, the bound alone decides.
A program may use at most 64 MiB of HBM per device.

v0:
```python
import math

import jax
import jax.numpy as jnp
from jax import lax
from jax.sharding import PartitionSpec as P

HIGH = lax.Precision.HIGHEST
TWO_PI = 2.0 * math.pi


def swapped(block, axis, distance):
    count = lax.axis_size(axis)
    route = []
    for low in range(count):
        high = low | 1 << distance
        if high != low and high < count:
            route += [(low, high), (high, low)]
    return lax.ppermute(block, axis, route)


def unit_circle(numer, denom):
    angle = TWO_PI * numer.astype(jnp.float32) / denom
    return (jnp.cos(angle), jnp.sin(angle))


def times(ar, ai, br, bi):
    return (ar * br - ai * bi, ar * bi + ai * br)


def dft_matrix(length, inverse):
    index = jnp.arange(length, dtype=jnp.int32)
    cosine, sine = unit_circle(index[:, None] * index[None, :] % length, length)
    if inverse:
        top = jnp.concatenate([cosine, sine], axis=1)
        bottom = jnp.concatenate([-sine, cosine], axis=1)
    else:
        top = jnp.concatenate([cosine, -sine], axis=1)
        bottom = jnp.concatenate([sine, cosine], axis=1)
    return jnp.concatenate([top, bottom], axis=0)


def along_time(real_part, imag_part, matrix):
    rows = real_part.shape[-1]
    stacked = jnp.concatenate([real_part, imag_part], axis=-1)
    result = jnp.dot(stacked, matrix, precision=HIGH)
    return (result[..., :rows], result[..., rows:])


def filter_terms(residues, decay_rates, length):
    lam = jnp.exp(-decay_rates)
    one_less = -jnp.expm1(-decay_rates)
    base = residues * jnp.sqrt(-jnp.expm1(-2.0 * decay_rates))
    tail = jnp.exp(-decay_rates * length)
    return (base, lam, one_less, tail)


def response(freq, total, filt):
    base, lam, one_less, tail = filt
    wrapped = freq % total
    cosine, sine = unit_circle(wrapped, total)
    half_sine = jnp.sin(math.pi * wrapped.astype(jnp.float32) / total)
    parity_sign = 1.0 - 2.0 * (wrapped % 2).astype(jnp.float32)
    resp_r = 0.0
    resp_i = 0.0
    for mode in range(base.shape[0]):
        numer = base[mode] * (1.0 - tail[mode] * parity_sign)
        den_r = one_less[mode] + 2.0 * lam[mode] * half_sine * half_sine
        den_i = lam[mode] * sine
        norm_sq = den_r * den_r + den_i * den_i
        resp_r = resp_r + numer * den_r / norm_sq
        resp_i = resp_i - numer * den_i / norm_sq
    return (resp_r, resp_i)


def spectral(spec_r, spec_i, q_index, filt, big_p, rows):
    total = 2 * big_p * rows
    fsel = jnp.arange(2, dtype=jnp.int32).reshape((2,) + (1,) * (spec_r.ndim - 1))
    freq = 2 * q_index + fsel
    pos = jnp.arange(rows, dtype=jnp.int32)
    cosine, sine = unit_circle(pos * freq % total, total)
    tw_r, tw_i = times(spec_r, spec_i, cosine, -sine)
    full_r, full_i = along_time(tw_r, tw_i, dft_matrix(rows, False))
    resp_r, resp_i = response(freq + 2 * big_p * pos, total, filt)
    prod_r, prod_i = times(full_r, full_i, resp_r, resp_i)
    back_r, back_i = along_time(prod_r, prod_i, dft_matrix(rows, True))
    return times(back_r, back_i, cosine, sine)


def pre_twiddle(mixed, p_index, big_p, shape_f):
    fsel = jnp.arange(2, dtype=jnp.int32).reshape(shape_f)
    cosine, sine = unit_circle(p_index * fsel % (2 * big_p), 2 * big_p)
    return (mixed * cosine, -mixed * sine)


def post_twiddle(spec_r, spec_i, p_index, big_p, rows, shape_f):
    fsel = jnp.arange(2, dtype=jnp.int32).reshape(shape_f)
    cosine, sine = unit_circle(p_index * fsel % (2 * big_p), 2 * big_p)
    return jnp.sum(cosine * spec_r - sine * spec_i, axis=0) / (2.0 * big_p * rows)


def reverse_bits(device, bits):
    result = jnp.zeros_like(device)
    for bit in range(bits):
        result = result | (device >> bit & 1) << bits - 1 - bit
    return result


def butterfly_forward(real_part, imag_part, device, bits):
    for bit in range(bits - 1, -1, -1):
        half = 1 << bit
        place = device % (2 * half)
        upper = place >= half
        other_r, other_i = swapped((real_part, imag_part), "ctx", bit)
        cosine, sine = unit_circle(jnp.where(upper, place - half, 0), 2 * half)
        tw_r, tw_i = times(other_r - real_part, other_i - imag_part, cosine, -sine)
        real_part = jnp.where(upper, tw_r, real_part + other_r)
        imag_part = jnp.where(upper, tw_i, imag_part + other_i)
    return (real_part, imag_part)


def butterfly_inverse(real_part, imag_part, device, bits):
    for bit in range(bits):
        half = 1 << bit
        place = device % (2 * half)
        upper = place >= half
        cosine, sine = unit_circle(jnp.where(upper, place - half, 0), 2 * half)
        tw_r, tw_i = times(real_part, imag_part, cosine, sine)
        send_r = jnp.where(upper, tw_r, real_part)
        send_i = jnp.where(upper, tw_i, imag_part)
        other_r, other_i = swapped((send_r, send_i), "ctx", bit)
        real_part = jnp.where(upper, other_r - tw_r, real_part + other_r)
        imag_part = jnp.where(upper, other_i - tw_i, imag_part + other_i)
    return (real_part, imag_part)


def on_device(gate_stream, key_stream, value_stream, residues, decay_rates, out_weight):
    big_p = lax.axis_size("ctx")
    bits = big_p.bit_length() - 1
    rows = key_stream.shape[0]
    length = float(big_p * rows)
    device = lax.axis_index("ctx")
    mixed = jnp.transpose(key_stream.astype(jnp.float32) * value_stream.astype(jnp.float32))
    base, lam, one_less, tail = filter_terms(residues, decay_rates, length)
    filt = (base[:, :, None], lam[:, :, None], one_less[:, :, None], tail[:, :, None])
    z_r, z_i = pre_twiddle(mixed, device, big_p, (2, 1, 1))
    y_r, y_i = butterfly_forward(z_r, z_i, device, bits)
    q_index = reverse_bits(device, bits)
    u_r, u_i = spectral(y_r, y_i, q_index, filt, big_p, rows)
    v_r, v_i = butterfly_inverse(u_r, u_i, device, bits)
    conv_t = post_twiddle(v_r, v_i, device, big_p, rows, (2, 1, 1))
    conv_rows = jnp.transpose(conv_t)
    gated = (gate_stream.astype(jnp.float32) * conv_rows).astype(jnp.bfloat16)
    partial_terms = jnp.dot(gated, out_weight, preferred_element_type=jnp.float32)
    return lax.psum_scatter(partial_terms, "chan", scatter_dimension=1, tiled=True).astype(
        jnp.bfloat16
    )


def solution(mesh):
    return jax.shard_map(
        on_device,
        mesh=mesh,
        in_specs=(
            P("ctx", "chan"),
            P("ctx", "chan"),
            P("ctx", "chan"),
            P(None, "chan"),
            P(None, "chan"),
            P("chan", None),
        ),
        out_specs=P("ctx", "chan"),
        check_vma=False,
    )
```

profile of v0, /device:TPU:27, one launch (start us, length us, event | category | flops | bytes accessed | tf_op | source)
XLA Modules:
  0.0 713.1 jit_solution(13681102103190333559)
XLA Ops:
  6.5 0.0 reduce-scatter.2.cloned.1.call-start
  6.5 0.1 fusion.99
  6.6 1.4 multiply_bitcast_fusion
  8.0 0.3 copy.12
  8.3 0.0 copy-start.1
  8.3 0.0 copy-start.2
  8.3 1.6 broadcast_multiply_fusion.1
  9.9 0.1 collective-permute-start
  10.0 0.1 fusion.98
  10.0 0.0 copy-done.2
  10.0 0.2 fusion.104
  10.2 0.3 copy.13
  10.6 1.6 broadcast_multiply_fusion
  12.2 2.3 collective-permute-start.1
  14.7 0.0 copy-start.4
  14.7 0.0 copy-start.5
  14.7 133.8 %collective-permute-done = f32[2,1024,256]{2,1,0:T(8,128)} collective-permute-done((f32[2,1024,256]{2,1,0:T(8,128)}, f32[2,1024,256]{2,1,0:T(8,128)}, u32[]{:S(2)}, u32[]{:S(2)}) %collective-permute-start) | collective-permute-done | bytes 2097184 | tf_op jit(solution)/shard_map/ppermute | solution.py:19
  148.5 44.9 %collective-permute-done.1 = f32[2,1024,256]{2,1,0:T(8,128)} collective-permute-done((f32[2,1024,256]{2,1,0:T(8,128)}, f32[2,1024,256]{2,1,0:T(8,128)}, u32[]{:S(2)}, u32[]{:S(2)}) %collective-permute-start.1) | collective-permute-done | bytes 2097184 | tf_op jit(solution)/shard_map/ppermute | solution.py:19
  193.4 5.3 add_select_fusion.8
  198.7 0.0 collective-permute-start.2
  198.7 1.5 collective-permute-start.3
  200.5 1.0 fusion.82
  201.6 0.2 fusion.90
  201.8 0.1 sqrt_multiply_fusion
  201.9 43.7 %collective-permute-done.2 = f32[2,1024,256]{2,1,0:T(8,128)S(1)} collective-permute-done((f32[2,1024,256]{2,1,0:T(8,128)}, f32[2,1024,256]{2,1,0:T(8,128)S(1)}, u32[]{:S(2)}, u32[]{:S(2)}) %collective-permute-start.2) | collective-permute-done | bytes 2097184 | tf_op jit(solution)/shard_map/ppermute | solution.py:19
  245.6 45.0 %collective-permute-done.3 = f32[2,1024,256]{2,1,0:T(8,128)} collective-permute-done((f32[2,1024,256]{2,1,0:T(8,128)}, f32[2,1024,256]{2,1,0:T(8,128)}, u32[]{:S(2)}, u32[]{:S(2)}) %collective-permute-start.3) | collective-permute-done | bytes 2097184 | tf_op jit(solution)/shard_map/ppermute | solution.py:19
  290.7 3.7 add_select_fusion.6
  294.4 1.4 collective-permute-start.4
  295.8 0.1 collective-permute-start.5
  295.9 1.0 fusion.84
  297.1 2.5 collective-permute-done.4
  299.6 3.0 collective-permute-done.5
  302.6 1.1 multiply_subtract_fusion.5
  303.7 0.3 multiply_add_fusion.21
  303.9 7.4 %fusion = f32[2,1024,512]{1,2,0:T(8,128)S(1)} fusion(f32[2,1024,256]{2,1,0:T(8,128)S(1)} %multiply_add_fusion.21, f32[2,1024,256]{2,1,0:T(8,128)S(1)} %get-tuple-element.17, f32[256,256]{0,1:T(8,128)S(1)} %get-tuple-element.99, f32[256,256]{0,1:T(8,128)S(1)} %get-tuple-element.98, f32[256,256]{0,1:T(8,128)S(1)} %fusion.84), kind=kOutput, calls=%fused_computation | convolution fusion | flops 6444285952 | bytes 9175040 | tf_op jit(solution)/shard_map/dot_general | solution.py:46
  311.3 22.7 %multiply_subtract_fusion.4 = (f32[2,1024,256]{1,2,0:T(8,128)S(1)}, f32[2,1024,256]{1,2,0:T(8,128)S(1)}, f32[2,1024,256]{1,2,0:T(8,128)S(1)}) fusion(f32[2,1024,512]{1,2,0:T(8,128)S(1)} %fusion, f32[1024]{0:T(1024)S(1)} %get-tuple-element.100, f32[1024]{0:T(1024)S(1)} %bitcast.145, f32[1024]{0:T(1024)S(1)} %bitcast.83, f32[1024]{0:T(1024)S(1)} %bitcast.129, ...), kind=kLoop, calls=%fused_computation.108 | loop fusion | flops 135266304 | bytes 10819584 | tf_op jit(solution)/shard_map/sub | solution.py:28
  334.0 1.0 multiply_add_fusion.4
  335.0 13.9 %fusion.4 = f32[2,1024,512]{2,1,0:T(8,128)S(1)} fusion(f32[2,1024,256]{1,2,0:T(8,128)S(1)} %multiply_add_fusion.4, f32[2,1024,256]{1,2,0:T(8,128)S(1)} %get-tuple-element.14, f32[256,256]{0,1:T(8,128)S(1)} %get-tuple-element.99, f32[256,256]{0,1:T(8,128)S(1)} %fusion.84, f32[256,256]{0,1:T(8,128)S(1)} %get-tuple-element.98), kind=kOutput, calls=%fused_computation.4 | convolution fusion | flops 6444285952 | bytes 9175040 | tf_op jit(solution)/shard_map/dot_general | solution.py:46
  348.9 0.8 fusion.61
  349.7 0.3 fusion.59
  350.0 0.4 collective-permute-start.7
  350.4 0.1 collective-permute-start.6
  350.5 3.7 collective-permute-done.7
  354.2 3.0 collective-permute-done.6
  357.2 1.1 fusion.60
  358.3 0.3 fusion.57
  358.6 0.1 collective-permute-start.9
  358.7 1.5 collective-permute-start.8
  360.1 45.4 %collective-permute-done.9 = f32[2,1024,256]{2,1,0:T(8,128)S(1)} collective-permute-done((f32[2,1024,256]{2,1,0:T(8,128)S(1)}, f32[2,1024,256]{2,1,0:T(8,128)S(1)}, u32[]{:S(2)}, u32[]{:S(2)}) %collective-permute-start.9) | collective-permute-done | bytes 2097184 | tf_op jit(solution)/shard_map/ppermute | solution.py:19
  405.5 44.9 %collective-permute-done.8 = f32[2,1024,256]{2,1,0:T(8,128)S(1)} collective-permute-done((f32[2,1024,256]{2,1,0:T(8,128)S(1)}, f32[2,1024,256]{2,1,0:T(8,128)S(1)}, u32[]{:S(2)}, u32[]{:S(2)}) %collective-permute-start.8) | collective-permute-done | bytes 2097184 | tf_op jit(solution)/shard_map/ppermute | solution.py:19
  450.4 2.5 fusion.58
  452.9 1.7 fusion.56
  454.6 0.4 copy-done
  454.9 0.0 collective-permute-start.11
  454.9 2.4 collective-permute-start.10
  457.3 0.0 copy-done.3
  457.3 0.2 copy.11
  457.5 135.8 %collective-permute-done.11 = f32[2,1024,256]{2,1,0:T(8,128)} collective-permute-done((f32[2,1024,256]{2,1,0:T(8,128)}, f32[2,1024,256]{2,1,0:T(8,128)}, u32[]{:S(2)}, u32[]{:S(2)}) %collective-permute-start.11) | collective-permute-done | bytes 2097184 | tf_op jit(solution)/shard_map/ppermute | solution.py:19
  593.3 44.9 %collective-permute-done.10 = f32[2,1024,256]{2,1,0:T(8,128)} collective-permute-done((f32[2,1024,256]{2,1,0:T(8,128)}, f32[2,1024,256]{2,1,0:T(8,128)}, u32[]{:S(2)}, u32[]{:S(2)}) %collective-permute-start.10) | collective-permute-done | bytes 2097184 | tf_op jit(solution)/shard_map/ppermute | solution.py:19
  638.3 4.1 subtract_reduce_fusion
  642.4 7.8 %fusion.73 = f32[256,4096]{1,0:T(8,128)} fusion(bf16[1024,4096]{1,0:T(8,128)(2,1)} %param.11, f32[1024,256]{1,0:T(8,128)S(1)} %subtract_reduce_fusion, bf16[256,1024]{0,1:T(8,128)(2,1)S(1)} %copy.11), kind=kOutput, calls=%fused_computation.169 | convolution fusion | flops 2148532224 | bytes 14155776 | tf_op jit(solution)/shard_map/dot_general | solution.py:154
  650.2 0.0 reduce-scatter.2.cloned.1.call-update
  650.2 53.5 %reduce-scatter.2.cloned.1.call-done = f32[256,1024]{1,0:T(8,128)} async-done(((f32[256,4096]{1,0:T(8,128)}), f32[256,1024]{1,0:T(8,128)}) %reduce-scatter.2.cloned.1.call-update) | async-done | bytes 1048592 | tf_op jit(solution)/shard_map/reduce_scatter | solution.py:155
  703.7 2.1 convert_element_type.103
  (19 shorter events, 0.3 us)
Async XLA Ops:
  6.5 697.2 %reduce-scatter.2.cloned.1.call-start = ((), (), s32[]{:S(2)}) async-start(), calls=%async_computation.1 | async-start | bytes 5242880 | tf_op jit(solution)/shard_map/reduce_scatter | solution.py:155
  8.3 1.7 copy-start.1
  8.3 1.7 copy-start.2
  9.9 138.5 %collective-permute-start = (f32[2,1024,256]{2,1,0:T(8,128)}, f32[2,1024,256]{2,1,0:T(8,128)}, u32[]{:S(2)}, u32[]{:S(2)}) collective-permute-start(f32[2,1024,256]{2,1,0:T(8,128)} %broadcast_multiply_fusion.1), channel_id=1, source_target_pairs={{0,4},{4,0},{1,5},{5,1},{2,6},{6,2},{3,7},{7,3},{8,12},{12,8},{9,1... | collective-permute-start | bytes 6291464 | tf_op jit(solution)/shard_map/ppermute | solution.py:19
  12.2 181.2 %collective-permute-start.1 = (f32[2,1024,256]{2,1,0:T(8,128)}, f32[2,1024,256]{2,1,0:T(8,128)}, u32[]{:S(2)}, u32[]{:S(2)}) collective-permute-start(f32[2,1024,256]{2,1,0:T(8,128)} %broadcast_multiply_fusion), channel_id=1, source_target_pairs={{0,4},{4,0},{1,5},{5,1},{2,6},{6,2},{3,7},{7,3},{8,12},{12,8},{9,1... | collective-permute-start | bytes 6291464 | tf_op jit(solution)/shard_map/ppermute | solution.py:19
  14.7 187.1 %copy-start.4 = (f32[16,1024]{1,0:T(8,128)S(1)}, f32[16,1024]{1,0:T(8,128)}, u32[]{:S(2)}) copy-start(f32[16,1024]{1,0:T(8,128)} %param.9) | copy-start | bytes 196612
  14.7 187.1 %copy-start.5 = (f32[16,1024]{1,0:T(8,128)S(1)}, f32[16,1024]{1,0:T(8,128)}, u32[]{:S(2)}) copy-start(f32[16,1024]{1,0:T(8,128)} %param.10) | copy-start | bytes 196612
  198.7 46.9 %collective-permute-start.2 = (f32[2,1024,256]{2,1,0:T(8,128)}, f32[2,1024,256]{2,1,0:T(8,128)S(1)}, u32[]{:S(2)}, u32[]{:S(2)}) collective-permute-start(f32[2,1024,256]{2,1,0:T(8,128)} %get-tuple-element.23), channel_id=1, source_target_pairs={{0,2},{2,0},{1,3},{3,1},{4,6},{6,4},{5,7},{7,5},{8,10},{10,8},{9,1... | collective-permute-start | bytes 6291464 | tf_op jit(solution)/shard_map/ppermute | solution.py:19
  198.7 92.0 %collective-permute-start.3 = (f32[2,1024,256]{2,1,0:T(8,128)}, f32[2,1024,256]{2,1,0:T(8,128)}, u32[]{:S(2)}, u32[]{:S(2)}) collective-permute-start(f32[2,1024,256]{2,1,0:T(8,128)} %get-tuple-element.22), channel_id=1, source_target_pairs={{0,2},{2,0},{1,3},{3,1},{4,6},{6,4},{5,7},{7,5},{8,10},{10,8},{9,1... | collective-permute-start | bytes 6291464 | tf_op jit(solution)/shard_map/ppermute | solution.py:19
  294.4 5.2 collective-permute-start.4
  295.8 6.8 collective-permute-start.5
  350.0 4.2 collective-permute-start.7
  350.4 6.8 collective-permute-start.6
  358.6 46.9 %collective-permute-start.9 = (f32[2,1024,256]{2,1,0:T(8,128)S(1)}, f32[2,1024,256]{2,1,0:T(8,128)S(1)}, u32[]{:S(2)}, u32[]{:S(2)}) collective-permute-start(f32[2,1024,256]{2,1,0:T(8,128)S(1)} %fusion.57), channel_id=1, source_target_pairs={{0,2},{2,0},{1,3},{3,1},{4,6},{6,4},{5,7},{7,5},{8,10},{10,8},{9,1... | collective-permute-start | bytes 6291464 | tf_op jit(solution)/shard_map/ppermute | solution.py:19
  358.7 91.8 %collective-permute-start.8 = (f32[2,1024,256]{2,1,0:T(8,128)S(1)}, f32[2,1024,256]{2,1,0:T(8,128)S(1)}, u32[]{:S(2)}, u32[]{:S(2)}) collective-permute-start(f32[2,1024,256]{2,1,0:T(8,128)S(1)} %get-tuple-element.8), channel_id=1, source_target_pairs={{0,2},{2,0},{1,3},{3,1},{4,6},{6,4},{5,7},{7,5},{8,10},{10,8},{9,1... | collective-permute-start | bytes 6291464 | tf_op jit(solution)/shard_map/ppermute | solution.py:19
  452.9 2.0 copy-start
  452.9 4.4 copy-start.3
  454.9 138.4 %collective-permute-start.11 = (f32[2,1024,256]{2,1,0:T(8,128)}, f32[2,1024,256]{2,1,0:T(8,128)}, u32[]{:S(2)}, u32[]{:S(2)}) collective-permute-start(f32[2,1024,256]{2,1,0:T(8,128)} %fusion.56), channel_id=1, source_target_pairs={{0,4},{4,0},{1,5},{5,1},{2,6},{6,2},{3,7},{7,3},{8,12},{12,8},{9,1... | collective-permute-start | bytes 6291464 | tf_op jit(solution)/shard_map/ppermute | solution.py:19
  454.9 183.3 %collective-permute-start.10 = (f32[2,1024,256]{2,1,0:T(8,128)}, f32[2,1024,256]{2,1,0:T(8,128)}, u32[]{:S(2)}, u32[]{:S(2)}) collective-permute-start(f32[2,1024,256]{2,1,0:T(8,128)} %get-tuple-element.5), channel_id=1, source_target_pairs={{0,4},{4,0},{1,5},{5,1},{2,6},{6,2},{3,7},{7,3},{8,12},{12,8},{9,1... | collective-permute-start | bytes 6291464 | tf_op jit(solution)/shard_map/ppermute | solution.py:19
Sparse Core Ops, SparseCore 0:
  650.3 53.3 reduce-scatter.1
where the time goes:
time: 724 us; the launch traced here: 713 us
  waiting for transfers between devices  604 us (83%)
  other arithmetic  53.9 us (7%)
  matrix products  29.1 us (4%)
  between operations  14.6 us (2%)
  starting transfers between devices  9.78 us (1%)
    ppermute x12, waiting for transfers between devices, swapped(): return lax.ppermute(block, axis, route)  551 us
    reduce_scatter x1, waiting for transfers between devices, on_device(): lax.psum_scatter(partial_terms, 'chan', scatter_dimension=1, tiled=True)  53.5 us
    sub x2, other arithmetic, times(): return (ar * br - ai * bi, ar * bi + ai * br)  23.8 us
    dot_general x2, matrix products, along_time(): result = jnp.dot(stacked, matrix, precision=HIGH)  21.3 us
  transfers between devices with their start and end apart: 13, of which 13 were waited for; matrix products, arithmetic and copies ran while one was open for 1% of the time, Pallas kernels for 0%

commit v1 on v0

--- a/solution.py
+++ b/solution.py
@@ -1,8 +1,11 @@
+import functools
 import math
 
 import jax
 import jax.numpy as jnp
 from jax import lax
+from jax.experimental import pallas as pl
+from jax.experimental.pallas import tpu as pltpu
 from jax.sharding import PartitionSpec as P
 
 HIGH = lax.Precision.HIGHEST
@@ -157,9 +160,328 @@
     )
 
 
+MESH = pl.DeviceIdType.MESH
+LANES = 128
+SUB = 8
+WIDE = 256
+CHUNKS = 16
+FORWARDS = 4
+
+
+def tree_sum(terms):
+    while len(terms) > 1:
+        pairs = [terms[i] + terms[i + 1] for i in range(0, len(terms) - 1, 2)]
+        terms = pairs + terms[len(pairs) * 2 :]
+    return terms[0]
+
+
+def one_minus_exp(u):
+    series = u * (1.0 - u / 2.0 * (1.0 - u / 3.0 * (1.0 - u / 4.0 * (1.0 - u / 5.0 * (1.0 - u / 6.0)))))
+    return jnp.where(u > 0.25, 1.0 - jnp.exp(-u), series)
+
+
+def kernel(
+    stages,
+    gate_hbm, key_hbm, value_hbm, res_hbm, decay_hbm, w_hbm, out_hbm,
+    gate, key, value, res, decay, wbuf, sbuf, rbuf, obuf, gated,
+    xs, ys, lam, base, dec, ends, give, chip, peer_end, zbuf, give_state, peer_state, state,
+    in_sem, w_sem, out_sem, chunk_send, chunk_recv, pair_send, pair_recv, z_send, z_recv,
+):
+    rows = gate.shape[0]
+    modes = res.shape[0]
+    half_modes = modes // 2
+    half_size = half_modes * SUB
+    chan = lax.axis_index("chan")
+    ctx = lax.axis_index("ctx")
+    core = lax.rem(ctx, 2)
+    stage = ctx // 2
+    x = lax.rem(chan, 2)
+    y = chan // 2
+    along_x = y * 2 + (1 - x)
+    along_y = (1 - y) * 2 + x
+    across = (1 - y) * 2 + (1 - x)
+    partner = stage * 2 + (1 - core)
+
+    loads = [
+        pltpu.make_async_copy(src, dst, in_sem.at[i])
+        for i, (src, dst) in enumerate(
+            [(key_hbm, key), (value_hbm, value), (decay_hbm, decay), (res_hbm, res), (gate_hbm, gate)]
+        )
+    ]
+    for load in loads:
+        load.start()
+
+    def w_copy(i):
+        owner = (across, along_y if i % 2 else along_x, along_x if i % 2 else along_y, chan)[i // 4]
+        column = owner * (4 * WIDE) + (i % 2) * 2 * WIDE + (i // 2 % 2) * WIDE
+        return pltpu.make_async_copy(
+            w_hbm.at[:, pl.ds(pl.multiple_of(column, WIDE), WIDE)], wbuf.at[i], w_sem.at[i]
+        )
+
+    for i in range(CHUNKS):
+        w_copy(i).start()
+
+    barrier = pltpu.get_barrier_semaphore()
+    pl.semaphore_signal(barrier, inc=1, device_id=(along_x, ctx), device_id_type=MESH)
+    pl.semaphore_signal(barrier, inc=1, device_id=(along_y, ctx), device_id_type=MESH)
+    pl.semaphore_signal(barrier, inc=1, device_id=(chan, partner), device_id_type=MESH)
+    for step in range(1, stages):
+        other = lax.rem(stage + step, stages) * 2 + core
+        pl.semaphore_signal(barrier, inc=1, device_id=(chan, other), device_id_type=MESH)
+
+    loads[2].wait()
+    loads[3].wait()
+    for b in range(SUB):
+        at = pl.ds(b, modes, stride=SUB)
+        d = decay[:, b * LANES : (b + 1) * LANES]
+        dec[at, :] = d
+        lam[at, :] = jnp.exp(-d)
+        base[at, :] = res[:, b * LANES : (b + 1) * LANES] * jnp.sqrt(one_minus_exp(2.0 * d))
+    loads[0].wait()
+    loads[1].wait()
+    for b in range(SUB):
+        cols = slice(b * LANES, (b + 1) * LANES)
+        xs[pl.ds(b, rows, stride=SUB), :] = key[:, cols].astype(jnp.float32) * value[:, cols].astype(jnp.float32)
+
+    def vec(t):
+        return pl.ds(pl.multiple_of(t * SUB, SUB), SUB)
+
+    def mode_rows(half, n):
+        return pl.ds(pl.multiple_of(half * half_size + n * SUB, SUB), SUB)
+
+    def half_rows(half):
+        return pl.ds(pl.multiple_of(half * half_size, half_size), half_size)
+
+    mid = rows // 2
+
+    def end_states(half, dst):
+        lams = [lam[mode_rows(half, n), :] for n in range(half_modes)]
+
+        def step(t, carry):
+            low, high = carry
+            x_low = xs[vec(t), :]
+            x_high = xs[vec(t + mid), :]
+            low = tuple(l * h + x_low for l, h in zip(lams, low))
+            high = tuple(l * h + x_high for l, h in zip(lams, high))
+            return (low, high)
+
+        zero = tuple(jnp.zeros((SUB, LANES), jnp.float32) for _ in range(half_modes))
+        low, high = lax.fori_loop(0, mid, step, (zero, zero), unroll=4)
+        for n in range(half_modes):
+            shrink = jnp.exp(dec[mode_rows(half, n), :] * float(-mid))
+            dst[n * SUB : (n + 1) * SUB, :] = shrink * low[n] + high[n]
+
+    end_states(1 - core, give)
+    pl.semaphore_wait(barrier, 3 + stages - 1)
+    send_end = pltpu.make_async_remote_copy(
+        src_ref=give, dst_ref=peer_end, send_sem=pair_send.at[0], recv_sem=pair_recv.at[0],
+        device_id=(chan, partner), device_id_type=MESH,
+    )
+    send_end.start()
+    end_states(core, ends)
+    send_end.wait_recv()
+
+    own_decay = dec[half_rows(core), :]
+    span = jnp.exp(own_decay * float(-rows))
+    is_first = core == 0
+    end_first = jnp.where(is_first, ends[...], peer_end[...])
+    end_second = jnp.where(is_first, peer_end[...], ends[...])
+    chip[...] = span * end_first + end_second
+
+    def push(step):
+        return pltpu.make_async_remote_copy(
+            src_ref=chip, dst_ref=zbuf.at[step - 1], send_sem=z_send.at[step - 1], recv_sem=z_recv.at[step - 1],
+            device_id=(chan, lax.rem(stage + step, stages) * 2 + core), device_id_type=MESH,
+        )
+
+    for step in range(1, stages):
+        @pl.when(stage + step < stages)
+        def _():
+            push(step).start()
+
+    lams = [lam[n * SUB : (n + 1) * SUB, :] for n in range(modes)]
+    bases = [base[n * SUB : (n + 1) * SUB, :] for n in range(modes)]
+
+    def local_step(t, hidden):
+        now = xs[vec(t), :]
+        hidden = tuple(l * h + now for l, h in zip(lams, hidden))
+        ys[vec(t), :] = tree_sum([b * h for b, h in zip(bases, hidden)])
+        return hidden
+
+    zero = tuple(jnp.zeros((SUB, LANES), jnp.float32) for _ in range(modes))
+    lax.fori_loop(0, rows, local_step, zero, unroll=4)
+
+    state[...] = jnp.zeros_like(state)
+    for step in range(1, stages):
+        @pl.when(stage >= step)
+        def _():
+            push(step).wait_recv()
+            weight = jnp.exp(dec[half_rows(core), :] * float(-2 * rows * (step - 1)))
+            state[...] += weight * zbuf[step - 1]
+
+    begin_first = state[...]
+    begin_second = span * begin_first + end_first
+    give_state[...] = jnp.where(is_first, begin_second, begin_first)
+    send_state = pltpu.make_async_remote_copy(
+        src_ref=give_state, dst_ref=peer_state, send_sem=pair_send.at[1], recv_sem=pair_recv.at[1],
+        device_id=(chan, partner), device_id_type=MESH,
+    )
+    send_state.start()
+    state[...] = jnp.where(is_first, begin_first, begin_second)
+
+    def add_state(half, src):
+        lams = [lam[mode_rows(half, n), :] for n in range(half_modes)]
+        low = tuple(base[mode_rows(half, n), :] * src[n * SUB : (n + 1) * SUB, :] for n in range(half_modes))
+        high = tuple(jnp.exp(dec[mode_rows(half, n), :] * float(-mid)) * low[n] for n in range(half_modes))
+
+        def step(t, carry):
+            low, high = carry
+            low = tuple(l * h for l, h in zip(lams, low))
+            high = tuple(l * h for l, h in zip(lams, high))
+            ys[vec(t), :] += tree_sum(list(low))
+            ys[vec(t + mid), :] += tree_sum(list(high))
+            return (low, high)
+
+        lax.fori_loop(0, mid, step, (low, high), unroll=4)
+
+    add_state(core, state)
+    send_state.wait_recv()
+    add_state(1 - core, peer_state)
+
+    loads[4].wait()
+    for b in range(SUB):
+        cols = slice(b * LANES, (b + 1) * LANES)
+        conv = ys[pl.ds(b, rows, stride=SUB), :]
+        gated[:, cols] = (gate[:, cols].astype(jnp.float32) * conv).astype(jnp.bfloat16)
+
+    def chunk_copy(i, target):
+        return pltpu.make_async_remote_copy(
+            src_ref=sbuf.at[i], dst_ref=rbuf.at[i], send_sem=chunk_send.at[i], recv_sem=chunk_recv.at[i],
+            device_id=(target, ctx), device_id_type=MESH,
+        )
+
+    def first_target(i):
+        odd = lax.rem(i, 2)
+        return along_x * (1 - odd) + along_y * odd
+
+    def second_target(i):
+        odd = lax.rem(i, 2)
+        return along_y * (1 - odd) + along_x * odd
+
+    @pl.loop(0, CHUNKS)
+    def _(i):
+        pltpu.make_async_copy(w_hbm.at[:, pl.ds(0, WIDE)], wbuf.at[i], w_sem.at[i]).wait()
+        sbuf[i] = jnp.dot(gated[...], wbuf[i], preferred_element_type=jnp.float32)
+
+        @pl.when(i < 2 * FORWARDS)
+        def _():
+            chunk_copy(i, first_target(i)).start()
+
+    @pl.loop(0, FORWARDS)
+    def _(j):
+        chunk_copy(j, first_target(j)).wait_recv()
+        sbuf[j + 2 * FORWARDS] += rbuf[j]
+        chunk_copy(j + 2 * FORWARDS, second_target(j)).start()
+
+    def out_copy(j):
+        column = lax.rem(j, 2) * (2 * WIDE) + (j // 2) * WIDE
+        return pltpu.make_async_copy(
+            obuf.at[j], out_hbm.at[:, pl.ds(pl.multiple_of(column, WIDE), WIDE)], out_sem.at[j]
+        )
+
+    @pl.loop(0, FORWARDS)
+    def _(j):
+        chunk_copy(j + FORWARDS, first_target(j)).wait_recv()
+        sbuf[j + 3 * FORWARDS] += rbuf[j + FORWARDS]
+
+    @pl.loop(0, FORWARDS)
+    def _(j):
+        chunk_copy(j + 2 * FORWARDS, second_target(j)).wait_recv()
+        obuf[j] = (sbuf[j + 3 * FORWARDS] + rbuf[j + 2 * FORWARDS]).astype(jnp.bfloat16)
+        out_copy(j).start()
+
+    send_end.wait_send()
+    send_state.wait_send()
+    for step in range(1, stages):
+        @pl.when(stage + step < stages)
+        def _():
+            push(step).wait_send()
+
+    @pl.loop(0, 2 * FORWARDS)
+    def _(i):
+        chunk_copy(i, first_target(i)).wait_send()
+
+    @pl.loop(0, FORWARDS)
+    def _(j):
+        chunk_copy(j + 2 * FORWARDS, second_target(j)).wait_send()
+        out_copy(j).wait()
+
+
+def fused(gate_stream, key_stream, value_stream, residues, decay_rates, out_weight):
+    rows, channels = gate_stream.shape
+    modes = residues.shape[0]
+    stages = lax.axis_size("ctx") // 2
+    f32, bf16 = jnp.float32, jnp.bfloat16
+    whole = (modes * SUB, LANES)
+    half = (modes // 2 * SUB, LANES)
+    dma = pltpu.SemaphoreType.DMA
+    return pl.pallas_call(
+        functools.partial(kernel, stages),
+        out_shape=jax.ShapeDtypeStruct((rows, 4 * WIDE), bf16),
+        in_specs=[pl.BlockSpec(memory_space=pl.ANY)] * 6,
+        out_specs=pl.BlockSpec(memory_space=pl.ANY),
+        scratch_shapes=[
+            pltpu.VMEM((rows, channels), bf16),
+            pltpu.VMEM((rows, channels), bf16),
+            pltpu.VMEM((rows, channels), bf16),
+            pltpu.VMEM((modes, channels), f32),
+            pltpu.VMEM((modes, channels), f32),
+            pltpu.VMEM((CHUNKS, channels, WIDE), bf16),
+            pltpu.VMEM((CHUNKS, rows, WIDE), f32),
+            pltpu.VMEM((3 * FORWARDS, rows, WIDE), f32),
+            pltpu.VMEM((FORWARDS, rows, WIDE), bf16),
+            pltpu.VMEM((rows, channels), bf16),
+            pltpu.VMEM((rows * SUB, LANES), f32),
+            pltpu.VMEM((rows * SUB, LANES), f32),
+            pltpu.VMEM(whole, f32),
+            pltpu.VMEM(whole, f32),
+            pltpu.VMEM(whole, f32),
+            pltpu.VMEM(half, f32),
+            pltpu.VMEM(half, f32),
+            pltpu.VMEM(half, f32),
+            pltpu.VMEM(half, f32),
+            pltpu.VMEM((stages - 1,) + half, f32),
+            pltpu.VMEM(half, f32),
+            pltpu.VMEM(half, f32),
+            pltpu.VMEM(half, f32),
+            dma((5,)),
+            dma((CHUNKS,)),
+            dma((FORWARDS,)),
+            dma((3 * FORWARDS,)),
+            dma((3 * FORWARDS,)),
+            dma((2,)),
+            dma((2,)),
+            dma((stages - 1,)),
+            dma((stages - 1,)),
+        ],
+        compiler_params=pltpu.CompilerParams(
+            collective_id=0, has_side_effects=True, vmem_limit_bytes=48 * 1024 * 1024
+        ),
+        cost_estimate=pl.CostEstimate(
+            flops=2 * rows * channels * 16 * WIDE, bytes_accessed=2 * channels * 16 * WIDE, transcendentals=0
+        ),
+    )(gate_stream, key_stream, value_stream, residues, decay_rates, out_weight)
+
+
+def run(*arrays):
+    square = lax.axis_size("chan") == 4 and lax.axis_size("ctx") % 2 == 0 and lax.axis_size("ctx") > 2
+    fits = arrays[0].shape[1] == SUB * LANES and arrays[5].shape[1] == 16 * WIDE
+    return (fused if square and fits else on_device)(*arrays)
+
+
 def solution(mesh):
     return jax.shard_map(
-        on_device,
+        run,
         mesh=mesh,
         in_specs=(
             P("ctx", "chan"),

time: 724 us -> 54.1 us (0.07); the launches traced: 713 us -> 53.7 us
  waiting for transfers between devices: 604 us -> 0 us
  other arithmetic: 53.9 us -> 0 us
  Pallas kernels: 0 us -> 48 us
  matrix products: 29.1 us -> 0 us
  between operations: 14.6 us -> 0.01 us
  starting transfers between devices: 9.78 us -> 0 us
    ppermute x12 -> x0, waiting for transfers between devices: 551 us -> none  [swapped(): return lax.ppermute(block, axis, route)]
    reduce_scatter x1 -> x0, waiting for transfers between devices: 53.5 us -> none  [on_device(): lax.psum_scatter(partial_terms, 'chan', scatter_dimension=1, tiled=True)]
    pallas_call x0 -> x1, Pallas kernels: none -> 48 us  [fused(): pl.pallas_call(functools.partial(kernel, stages), out_shape=jax.ShapeDtyp...]
    dot_general x3 -> x0, matrix products: 29.1 us -> none  [the longest x2 21.3 us: along_time(): result = jnp.dot(stacked, matrix, precision=HIGH)]
    sub x3 -> x0, other arithmetic: 24 us -> none  [the longest x2 23.8 us: times(): return (ar * br - ai * bi, ar * bi + ai * br)]
    select_n x8 -> x0, other arithmetic: 15.5 us -> none  [the longest x2 9.02 us: butterfly_forward(): imag_part = jnp.where(upper, tw_i, imag_part + other_i)]
    ppermute x12 -> x0, starting transfers between devices: 9.78 us -> none  [swapped(): return lax.ppermute(block, axis, route)]
  transfers between devices with their start and end apart: 13 -> 0, of which waited for: 13 -> 0; matrix products, arithmetic and copies ran while one was open for 1% -> 0% of each run, Pallas kernels for 0% -> 0%
where the time goes in v1:
time: 54.1 us; the launch traced here: 53.7 us
  Pallas kernels  48 us (89%)
  local copies, waits for them, and re-layouts  5.6 us (10%)
    pallas_call x1, Pallas kernels, fused(): pl.pallas_call(functools.partial(kernel, stages), out_shape=jax.ShapeDtyp...  48 us
    unnamed x11, local copies, waits for them, and re-layouts  5.6 us

profile of v1, /device:TPU:27, one launch (start us, length us, event | category | flops | bytes accessed | tf_op | source)
XLA Modules:
  0.0 53.7 jit_solution(4610685143729311262)
XLA Ops:
  0.0 0.0 copy-start
  0.0 1.0 %copy-done = bf16[256,1024]{1,0:T(8,128)(2,1)S(1)} copy-done((bf16[256,1024]{1,0:T(8,128)(2,1)S(1)}, bf16[256,1024]{1,0:T(8,128)(2,1)}, u32[]{:S(2)}) %copy-start) | copy-done | bytes 524312
  1.0 0.0 copy-start.1
  1.0 1.0 %copy-done.1 = bf16[256,1024]{1,0:T(8,128)(2,1)S(1)} copy-done((bf16[256,1024]{1,0:T(8,128)(2,1)S(1)}, bf16[256,1024]{1,0:T(8,128)(2,1)}, u32[]{:S(2)}) %copy-start.1) | copy-done | bytes 524312
  2.1 0.0 copy-start.2
  2.1 1.0 %copy-done.2 = bf16[256,1024]{1,0:T(8,128)(2,1)S(1)} copy-done((bf16[256,1024]{1,0:T(8,128)(2,1)S(1)}, bf16[256,1024]{1,0:T(8,128)(2,1)}, u32[]{:S(2)}) %copy-start.2) | copy-done | bytes 524312
  3.1 0.0 copy-start.3
  3.1 0.8 %copy-done.3 = f32[16,1024]{1,0:T(8,128)S(1)} copy-done((f32[16,1024]{1,0:T(8,128)S(1)}, f32[16,1024]{1,0:T(8,128)}, u32[]{:S(2)}) %copy-start.3) | copy-done | bytes 65560
  4.0 0.0 copy-start.4
  4.0 0.8 %copy-done.4 = f32[16,1024]{1,0:T(8,128)S(1)} copy-done((f32[16,1024]{1,0:T(8,128)S(1)}, f32[16,1024]{1,0:T(8,128)}, u32[]{:S(2)}) %copy-start.4) | copy-done | bytes 65560
  4.8 48.0 %shard_map.64 = bf16[256,1024]{1,0:T(8,128)(2,1)S(1)} custom-call(bf16[256,1024]{1,0:T(8,128)(2,1)S(1)} %copy-done, bf16[256,1024]{1,0:T(8,128)(2,1)S(1)} %copy-done.1, bf16[256,1024]{1,0:T(8,128)(2,1)S(1)} %copy-done.2, f32[16,1024]{1,0:T(8,128)S(1)} %copy-done.3, f32[16,1024]{1,0:T(8,128)S(1)} %copy-done.4, bf16[1024,4096]{1,0:T(8,128)(2,1)} %w_hbm.1), custom_call_target="tpu_custom_call" | custom-call | flops 2147483648 | bytes 8388608 | tf_op jit(solution)/shard_map/pallas_call | solution.py:428
  52.9 0.8 %copy.8 = bf16[256,1024]{1,0:T(8,128)(2,1)} copy(bf16[256,1024]{1,0:T(8,128)(2,1)S(1)} %shard_map.64) | data formatting | bytes 1048576
Async XLA Ops:
  0.0 1.0 %copy-start = (bf16[256,1024]{1,0:T(8,128)(2,1)S(1)}, bf16[256,1024]{1,0:T(8,128)(2,1)}, u32[]{:S(2)}) copy-start(bf16[256,1024]{1,0:T(8,128)(2,1)} %gate_hbm.1) | copy-start | bytes 1572868
  1.0 1.0 %copy-start.1 = (bf16[256,1024]{1,0:T(8,128)(2,1)S(1)}, bf16[256,1024]{1,0:T(8,128)(2,1)}, u32[]{:S(2)}) copy-start(bf16[256,1024]{1,0:T(8,128)(2,1)} %key_hbm.1) | copy-start | bytes 1572868
  2.1 1.0 %copy-start.2 = (bf16[256,1024]{1,0:T(8,128)(2,1)S(1)}, bf16[256,1024]{1,0:T(8,128)(2,1)}, u32[]{:S(2)}) copy-start(bf16[256,1024]{1,0:T(8,128)(2,1)} %value_hbm.1) | copy-start | bytes 1572868
  3.1 0.8 %copy-start.3 = (f32[16,1024]{1,0:T(8,128)S(1)}, f32[16,1024]{1,0:T(8,128)}, u32[]{:S(2)}) copy-start(f32[16,1024]{1,0:T(8,128)} %res_hbm.1) | copy-start | bytes 196612
  4.0 0.8 %copy-start.4 = (f32[16,1024]{1,0:T(8,128)S(1)}, f32[16,1024]{1,0:T(8,128)}, u32[]{:S(2)}) copy-start(f32[16,1024]{1,0:T(8,128)} %decay_hbm.1) | copy-start | bytes 196612

commit v2 on v1

--- a/solution.py
+++ b/solution.py
@@ -163,9 +163,10 @@
 MESH = pl.DeviceIdType.MESH
 LANES = 128
 SUB = 8
-WIDE = 256
+WIDE = 512
 CHUNKS = 16
 FORWARDS = 4
+SLABS = 4
 
 
 def tree_sum(terms):
@@ -205,21 +206,27 @@
     loads = [
         pltpu.make_async_copy(src, dst, in_sem.at[i])
         for i, (src, dst) in enumerate(
-            [(key_hbm, key), (value_hbm, value), (decay_hbm, decay), (res_hbm, res), (gate_hbm, gate)]
+            [(decay_hbm, decay), (res_hbm, res), (gate_hbm, gate)]
         )
     ]
-    for load in loads:
+    slab = rows // SLABS
+
+    def stream_load(i):
+        src, dst = (key_hbm, key) if i % 2 == 0 else (value_hbm, value)
+        here = pl.ds(i // 2 * slab, slab)
+        return pltpu.make_async_copy(src.at[here, :], dst.at[here, :], in_sem.at[3 + i])
+
+    for i in range(2 * SLABS):
+        stream_load(i).start()
+    for load in loads[:2]:
         load.start()
 
     def w_copy(i):
-        owner = (across, along_y if i % 2 else along_x, along_x if i % 2 else along_y, chan)[i // 4]
-        column = owner * (4 * WIDE) + (i % 2) * 2 * WIDE + (i // 2 % 2) * WIDE
+        owner = (across, along_y if i % 2 else along_x, along_x if i % 2 else along_y, chan)[i // 2]
+        column = owner * (2 * WIDE) + (i % 2) * WIDE
         return pltpu.make_async_copy(
             w_hbm.at[:, pl.ds(pl.multiple_of(column, WIDE), WIDE)], wbuf.at[i], w_sem.at[i]
         )
-
-    for i in range(CHUNKS):
-        w_copy(i).start()
 
     barrier = pltpu.get_barrier_semaphore()
     pl.semaphore_signal(barrier, inc=1, device_id=(along_x, ctx), device_id_type=MESH)
@@ -229,19 +236,25 @@
         other = lax.rem(stage + step, stages) * 2 + core
         pl.semaphore_signal(barrier, inc=1, device_id=(chan, other), device_id_type=MESH)
 
-    loads[2].wait()
-    loads[3].wait()
+    loads[0].wait()
+    loads[1].wait()
     for b in range(SUB):
         at = pl.ds(b, modes, stride=SUB)
         d = decay[:, b * LANES : (b + 1) * LANES]
         dec[at, :] = d
         lam[at, :] = jnp.exp(-d)
         base[at, :] = res[:, b * LANES : (b + 1) * LANES] * jnp.sqrt(one_minus_exp(2.0 * d))
-    loads[0].wait()
-    loads[1].wait()
-    for b in range(SUB):
-        cols = slice(b * LANES, (b + 1) * LANES)
-        xs[pl.ds(b, rows, stride=SUB), :] = key[:, cols].astype(jnp.float32) * value[:, cols].astype(jnp.float32)
+    for part in range(SLABS):
+        stream_load(2 * part).wait()
+        stream_load(2 * part + 1).wait()
+        here = slice(part * slab, (part + 1) * slab)
+        for b in range(SUB):
+            cols = slice(b * LANES, (b + 1) * LANES)
+            mixed = key[here, cols].astype(jnp.float32) * value[here, cols].astype(jnp.float32)
+            xs[pl.ds(part * slab * SUB + b, slab, stride=SUB), :] = mixed
+    loads[2].start()
+    for i in range(CHUNKS // 2):
+        w_copy(i).start()
 
     def vec(t):
         return pl.ds(pl.multiple_of(t * SUB, SUB), SUB)
@@ -329,30 +342,34 @@
     send_state.start()
     state[...] = jnp.where(is_first, begin_first, begin_second)
 
-    def add_state(half, src):
+    quarter = rows // 4
+
+    def add_state(half, src, part):
         lams = [lam[mode_rows(half, n), :] for n in range(half_modes)]
-        low = tuple(base[mode_rows(half, n), :] * src[n * SUB : (n + 1) * SUB, :] for n in range(half_modes))
-        high = tuple(jnp.exp(dec[mode_rows(half, n), :] * float(-mid)) * low[n] for n in range(half_modes))
+        start = part * mid
+        low, high = [], []
+        for n in range(half_modes):
+            d = dec[mode_rows(half, n), :]
+            first = base[mode_rows(half, n), :] * src[n * SUB : (n + 1) * SUB, :]
+            low.append(first * jnp.exp(d * float(-start)) if part else first)
+            high.append(first * jnp.exp(d * float(-start - quarter)))
 
         def step(t, carry):
             low, high = carry
             low = tuple(l * h for l, h in zip(lams, low))
             high = tuple(l * h for l, h in zip(lams, high))
-            ys[vec(t), :] += tree_sum(list(low))
-            ys[vec(t + mid), :] += tree_sum(list(high))
+            ys[vec(t + start), :] += tree_sum(list(low))
+            ys[vec(t + start + quarter), :] += tree_sum(list(high))
             return (low, high)
 
-        lax.fori_loop(0, mid, step, (low, high), unroll=4)
-
-    add_state(core, state)
-    send_state.wait_recv()
-    add_state(1 - core, peer_state)
-
-    loads[4].wait()
-    for b in range(SUB):
-        cols = slice(b * LANES, (b + 1) * LANES)
-        conv = ys[pl.ds(b, rows, stride=SUB), :]
-        gated[:, cols] = (gate[:, cols].astype(jnp.float32) * conv).astype(jnp.bfloat16)
+        lax.fori_loop(0, quarter, step, (tuple(low), tuple(high)), unroll=4)
+
+    def gate_rows(part):
+        here = slice(part * mid, (part + 1) * mid)
+        for b in range(SUB):
+            cols = slice(b * LANES, (b + 1) * LANES)
+            conv = ys[pl.ds(part * mid * SUB + b, mid, stride=SUB), :]
+            gated[here, cols] = (gate[here, cols].astype(jnp.float32) * conv).astype(jnp.bfloat16)
 
     def chunk_copy(i, target):
         return pltpu.make_async_remote_copy(
@@ -368,10 +385,40 @@
         odd = lax.rem(i, 2)
         return along_y * (1 - odd) + along_x * odd
 
-    @pl.loop(0, CHUNKS)
+    def w_wait(i):
+        pltpu.make_async_copy(w_hbm.at[:, pl.ds(0, WIDE)], wbuf.at[i], w_sem.at[i]).wait()
+
+    def block_of(i):
+        return i // 4 * 2 + lax.rem(i, 2)
+
+    def partial_sum(i):
+        part = lax.rem(i // 2, 2)
+        here = pl.ds(pl.multiple_of(part * mid, mid), mid)
+        sbuf[i] = jnp.dot(gated[here, :], wbuf[block_of(i)], preferred_element_type=jnp.float32)
+
+    add_state(core, state, 0)
+    send_state.wait_recv()
+    add_state(1 - core, peer_state, 0)
+    loads[2].wait()
+    gate_rows(0)
+
+    @pl.loop(0, 2)
     def _(i):
-        pltpu.make_async_copy(w_hbm.at[:, pl.ds(0, WIDE)], wbuf.at[i], w_sem.at[i]).wait()
-        sbuf[i] = jnp.dot(gated[...], wbuf[i], preferred_element_type=jnp.float32)
+        w_wait(i)
+        partial_sum(i)
+        chunk_copy(i, first_target(i)).start()
+
+    add_state(core, state, 1)
+    add_state(1 - core, peer_state, 1)
+    gate_rows(1)
+
+    @pl.loop(2, CHUNKS)
+    def _(i):
+        @pl.when(lax.rem(i // 2, 2) == 0)
+        def _():
+            w_wait(block_of(i))
+
+        partial_sum(i)
 
         @pl.when(i < 2 * FORWARDS)
         def _():
@@ -384,10 +431,9 @@
         chunk_copy(j + 2 * FORWARDS, second_target(j)).start()
 
     def out_copy(j):
-        column = lax.rem(j, 2) * (2 * WIDE) + (j // 2) * WIDE
-        return pltpu.make_async_copy(
-            obuf.at[j], out_hbm.at[:, pl.ds(pl.multiple_of(column, WIDE), WIDE)], out_sem.at[j]
-        )
+        here = pl.ds(pl.multiple_of(j // 2 * mid, mid), mid)
+        cols = pl.ds(pl.multiple_of(lax.rem(j, 2) * WIDE, WIDE), WIDE)
+        return pltpu.make_async_copy(obuf.at[j], out_hbm.at[here, cols], out_sem.at[j])
 
     @pl.loop(0, FORWARDS)
     def _(j):
@@ -427,19 +473,19 @@
     dma = pltpu.SemaphoreType.DMA
     return pl.pallas_call(
         functools.partial(kernel, stages),
-        out_shape=jax.ShapeDtypeStruct((rows, 4 * WIDE), bf16),
-        in_specs=[pl.BlockSpec(memory_space=pl.ANY)] * 6,
-        out_specs=pl.BlockSpec(memory_space=pl.ANY),
+        out_shape=jax.ShapeDtypeStruct((rows, 2 * WIDE), bf16),
+        in_specs=[pl.BlockSpec(memory_space=pltpu.HBM)] * 6,
+        out_specs=pl.BlockSpec(memory_space=pltpu.HBM),
         scratch_shapes=[
             pltpu.VMEM((rows, channels), bf16),
             pltpu.VMEM((rows, channels), bf16),
             pltpu.VMEM((rows, channels), bf16),
             pltpu.VMEM((modes, channels), f32),
             pltpu.VMEM((modes, channels), f32),
-            pltpu.VMEM((CHUNKS, channels, WIDE), bf16),
-            pltpu.VMEM((CHUNKS, rows, WIDE), f32),
-            pltpu.VMEM((3 * FORWARDS, rows, WIDE), f32),
-            pltpu.VMEM((FORWARDS, rows, WIDE), bf16),
+            pltpu.VMEM((CHUNKS // 2, channels, WIDE), bf16),
+            pltpu.VMEM((CHUNKS, rows // 2, WIDE), f32),
+            pltpu.VMEM((3 * FORWARDS, rows // 2, WIDE), f32),
+            pltpu.VMEM((FORWARDS, rows // 2, WIDE), bf16),
             pltpu.VMEM((rows, channels), bf16),
             pltpu.VMEM((rows * SUB, LANES), f32),
             pltpu.VMEM((rows * SUB, LANES), f32),
@@ -454,8 +500,8 @@
             pltpu.VMEM(half, f32),
             pltpu.VMEM(half, f32),
             pltpu.VMEM(half, f32),
-            dma((5,)),
-            dma((CHUNKS,)),
+            dma((3 + 2 * SLABS,)),
+            dma((CHUNKS // 2,)),
             dma((FORWARDS,)),
             dma((3 * FORWARDS,)),
             dma((3 * FORWARDS,)),
@@ -465,17 +511,17 @@
             dma((stages - 1,)),
         ],
         compiler_params=pltpu.CompilerParams(
-            collective_id=0, has_side_effects=True, vmem_limit_bytes=48 * 1024 * 1024
+            collective_id=0, has_side_effects=True, vmem_limit_bytes=64 * 1024 * 1024
         ),
         cost_estimate=pl.CostEstimate(
-            flops=2 * rows * channels * 16 * WIDE, bytes_accessed=2 * channels * 16 * WIDE, transcendentals=0
+            flops=2 * rows * channels * 8 * WIDE, bytes_accessed=2 * channels * 8 * WIDE, transcendentals=0
         ),
     )(gate_stream, key_stream, value_stream, residues, decay_rates, out_weight)
 
 
 def run(*arrays):
     square = lax.axis_size("chan") == 4 and lax.axis_size("ctx") % 2 == 0 and lax.axis_size("ctx") > 2
-    fits = arrays[0].shape[1] == SUB * LANES and arrays[5].shape[1] == 16 * WIDE
+    fits = arrays[0].shape[1] == SUB * LANES and arrays[5].shape[1] == 8 * WIDE
     return (fused if square and fits else on_device)(*arrays)
 
 

time: 54.1 us -> 50 us (0.924)
  local copies, waits for them, and re-layouts: 5.6 us -> 1.87 us
    unnamed x11 -> x1, local copies, waits for them, and re-layouts: 5.6 us -> 1.87 us
where the time goes in v2:
time: 50 us; the launch traced here: 49.7 us
  Pallas kernels  47.9 us (96%)
  local copies, waits for them, and re-layouts  1.87 us (4%)
    pallas_call x1, Pallas kernels, fused(): pl.pallas_call(functools.partial(kernel, stages), out_shape=jax.ShapeDtyp...  47.9 us
    unnamed x1, local copies, waits for them, and re-layouts  1.87 us

profile of v2, /device:TPU:27, one launch (start us, length us, event | category | flops | bytes accessed | tf_op | source)
XLA Modules:
  0.0 49.7 jit_solution(2551861235101370612)
XLA Ops:
  0.0 47.9 %shard_map.64 = bf16[256,1024]{1,0:T(8,128)(2,1)} custom-call(bf16[256,1024]{1,0:T(8,128)(2,1)} %gate_hbm.1, bf16[256,1024]{1,0:T(8,128)(2,1)} %key_hbm.1, bf16[256,1024]{1,0:T(8,128)(2,1)} %value_hbm.1, f32[16,1024]{1,0:T(8,128)} %res_hbm.1, f32[16,1024]{1,0:T(8,128)} %decay_hbm.1, bf16[1024,4096]{1,0:T(8,128)(2,1)} %w_hbm.1), custom_call_target="tpu_custom_call" | custom-call | flops 2147483648 | bytes 8388608 | tf_op jit(solution)/shard_map/pallas_call | solution.py:474
  47.9 1.9 %copy.8 = bf16[256,1024]{1,0:T(8,128)(2,1)} copy(bf16[256,1024]{1,0:T(8,128)(2,1)} %shard_map.64) | data formatting | bytes 1048576

commit v3 on v2

--- a/solution.py
+++ b/solution.py
@@ -183,10 +183,10 @@
 
 def kernel(
     stages,
-    gate_hbm, key_hbm, value_hbm, res_hbm, decay_hbm, w_hbm, out_hbm,
-    gate, key, value, res, decay, wbuf, sbuf, rbuf, obuf, gated,
+    gate_hbm, key_hbm, value_hbm, res_hbm, decay_hbm, w_hbm, out,
+    gate, key, value, res, decay, wbuf, sbuf, rbuf, gated,
     xs, ys, lam, base, dec, ends, give, chip, peer_end, zbuf, give_state, peer_state, state,
-    in_sem, w_sem, out_sem, chunk_send, chunk_recv, pair_send, pair_recv, z_send, z_recv,
+    in_sem, w_sem, chunk_send, chunk_recv, pair_send, pair_recv, z_send, z_recv,
 ):
     rows = gate.shape[0]
     modes = res.shape[0]
@@ -420,9 +420,14 @@
 
         partial_sum(i)
 
-        @pl.when(i < 2 * FORWARDS)
+        @pl.when(i < FORWARDS)
         def _():
             chunk_copy(i, first_target(i)).start()
+
+    @pl.loop(0, FORWARDS)
+    def _(j):
+        chunk_copy(j, first_target(j)).wait_send()
+        chunk_copy(j + FORWARDS, first_target(j)).start()
 
     @pl.loop(0, FORWARDS)
     def _(j):
@@ -430,11 +435,6 @@
         sbuf[j + 2 * FORWARDS] += rbuf[j]
         chunk_copy(j + 2 * FORWARDS, second_target(j)).start()
 
-    def out_copy(j):
-        here = pl.ds(pl.multiple_of(j // 2 * mid, mid), mid)
-        cols = pl.ds(pl.multiple_of(lax.rem(j, 2) * WIDE, WIDE), WIDE)
-        return pltpu.make_async_copy(obuf.at[j], out_hbm.at[here, cols], out_sem.at[j])
-
     @pl.loop(0, FORWARDS)
     def _(j):
         chunk_copy(j + FORWARDS, first_target(j)).wait_recv()
@@ -443,8 +443,9 @@
     @pl.loop(0, FORWARDS)
     def _(j):
         chunk_copy(j + 2 * FORWARDS, second_target(j)).wait_recv()
-        obuf[j] = (sbuf[j + 3 * FORWARDS] + rbuf[j + 2 * FORWARDS]).astype(jnp.bfloat16)
-        out_copy(j).start()
+        here = pl.ds(pl.multiple_of(j // 2 * mid, mid), mid)
+        cols = pl.ds(pl.multiple_of(lax.rem(j, 2) * WIDE, WIDE), WIDE)
+        out[here, cols] = (sbuf[j + 3 * FORWARDS] + rbuf[j + 2 * FORWARDS]).astype(jnp.bfloat16)
 
     send_end.wait_send()
     send_state.wait_send()
@@ -453,14 +454,10 @@
         def _():
             push(step).wait_send()
 
-    @pl.loop(0, 2 * FORWARDS)
-    def _(i):
-        chunk_copy(i, first_target(i)).wait_send()
-
     @pl.loop(0, FORWARDS)
     def _(j):
+        chunk_copy(j + FORWARDS, first_target(j)).wait_send()
         chunk_copy(j + 2 * FORWARDS, second_target(j)).wait_send()
-        out_copy(j).wait()
 
 
 def fused(gate_stream, key_stream, value_stream, residues, decay_rates, out_weight):
@@ -473,9 +470,9 @@
     dma = pltpu.SemaphoreType.DMA
     return pl.pallas_call(
         functools.partial(kernel, stages),
-        out_shape=jax.ShapeDtypeStruct((rows, 2 * WIDE), bf16),
+        out_shape=pltpu.VMEM((rows, 2 * WIDE), bf16),
         in_specs=[pl.BlockSpec(memory_space=pltpu.HBM)] * 6,
-        out_specs=pl.BlockSpec(memory_space=pltpu.HBM),
+        out_specs=pl.BlockSpec(memory_space=pltpu.VMEM),
         scratch_shapes=[
             pltpu.VMEM((rows, channels), bf16),
             pltpu.VMEM((rows, channels), bf16),
@@ -485,7 +482,6 @@
             pltpu.VMEM((CHUNKS // 2, channels, WIDE), bf16),
             pltpu.VMEM((CHUNKS, rows // 2, WIDE), f32),
             pltpu.VMEM((3 * FORWARDS, rows // 2, WIDE), f32),
-            pltpu.VMEM((FORWARDS, rows // 2, WIDE), bf16),
             pltpu.VMEM((rows, channels), bf16),
             pltpu.VMEM((rows * SUB, LANES), f32),
             pltpu.VMEM((rows * SUB, LANES), f32),
@@ -502,7 +498,6 @@
             pltpu.VMEM(half, f32),
             dma((3 + 2 * SLABS,)),
             dma((CHUNKS // 2,)),
-            dma((FORWARDS,)),
             dma((3 * FORWARDS,)),
             dma((3 * FORWARDS,)),
             dma((2,)),
@@ -511,7 +506,7 @@
             dma((stages - 1,)),
         ],
         compiler_params=pltpu.CompilerParams(
-            collective_id=0, has_side_effects=True, vmem_limit_bytes=64 * 1024 * 1024
+            collective_id=0, has_side_effects=True, vmem_limit_bytes=63 * 1024 * 1024
         ),
         cost_estimate=pl.CostEstimate(
             flops=2 * rows * channels * 8 * WIDE, bytes_accessed=2 * channels * 8 * WIDE, transcendentals=0

time: 50 us -> 48.2 us (0.964)
  local copies, waits for them, and re-layouts: 1.87 us -> 0.8 us
  Pallas kernels: 47.9 us -> 47.2 us
    unnamed x1, local copies, waits for them, and re-layouts: 1.87 us -> 0.8 us
    pallas_call x1, Pallas kernels: 47.9 us -> 47.2 us  [fused(): pl.pallas_call(functools.partial(kernel, stages), out_shape=pltpu.VMEM((r...]
where the time goes in v3:
time: 48.2 us; the launch traced here: 48 us
  Pallas kernels  47.2 us (98%)
  local copies, waits for them, and re-layouts  0.8 us (2%)
    pallas_call x1, Pallas kernels, fused(): pl.pallas_call(functools.partial(kernel, stages), out_shape=pltpu.VMEM((r...  47.2 us

profile of v3, /device:TPU:27, one launch (start us, length us, event | category | flops | bytes accessed | tf_op | source)
XLA Modules:
  0.0 48.0 jit_solution(4971828825386279477)
XLA Ops:
  0.0 47.2 %shard_map.64 = bf16[256,1024]{1,0:T(8,128)(2,1)S(1)} custom-call(bf16[256,1024]{1,0:T(8,128)(2,1)} %gate_hbm.1, bf16[256,1024]{1,0:T(8,128)(2,1)} %key_hbm.1, bf16[256,1024]{1,0:T(8,128)(2,1)} %value_hbm.1, f32[16,1024]{1,0:T(8,128)} %res_hbm.1, f32[16,1024]{1,0:T(8,128)} %decay_hbm.1, bf16[1024,4096]{1,0:T(8,128)(2,1)} %w_hbm.1), custom_call_target="tpu_custom_call" | custom-call | flops 2147483648 | bytes 8388608 | tf_op jit(solution)/shard_map/pallas_call | solution.py:471
  47.2 0.8 %copy.8 = bf16[256,1024]{1,0:T(8,128)(2,1)} copy(bf16[256,1024]{1,0:T(8,128)(2,1)S(1)} %shard_map.64) | data formatting | bytes 1048576

commit v4 on v3

--- a/solution.py
+++ b/solution.py
@@ -185,7 +185,7 @@
     stages,
     gate_hbm, key_hbm, value_hbm, res_hbm, decay_hbm, w_hbm, out,
     gate, key, value, res, decay, wbuf, sbuf, rbuf, gated,
-    xs, ys, lam, base, dec, ends, give, chip, peer_end, zbuf, give_state, peer_state, state,
+    xs, ys, lam, base, dec, carried, ends, give, chip, peer_end, zbuf, give_state, peer_state, state,
     in_sem, w_sem, chunk_send, chunk_recv, pair_send, pair_recv, z_send, z_recv,
 ):
     rows = gate.shape[0]
@@ -312,18 +312,26 @@
         def _():
             push(step).start()
 
-    lams = [lam[n * SUB : (n + 1) * SUB, :] for n in range(modes)]
-    bases = [base[n * SUB : (n + 1) * SUB, :] for n in range(modes)]
-
-    def local_step(t, hidden):
-        now = xs[vec(t), :]
-        hidden = tuple(l * h + now for l, h in zip(lams, hidden))
-        ys[vec(t), :] = tree_sum([b * h for b, h in zip(bases, hidden)])
-        return hidden
-
-    zero = tuple(jnp.zeros((SUB, LANES), jnp.float32) for _ in range(modes))
-    lax.fori_loop(0, rows, local_step, zero, unroll=4)
-
+    def local_rows(part):
+        lams = [lam[n * SUB : (n + 1) * SUB, :] for n in range(modes)]
+        bases = [base[n * SUB : (n + 1) * SUB, :] for n in range(modes)]
+
+        def step(t, hidden):
+            now = xs[vec(t), :]
+            hidden = tuple(l * h + now for l, h in zip(lams, hidden))
+            ys[vec(t), :] = tree_sum([b * h for b, h in zip(bases, hidden)])
+            return hidden
+
+        if part:
+            start = tuple(carried[n * SUB : (n + 1) * SUB, :] for n in range(modes))
+        else:
+            start = tuple(jnp.zeros((SUB, LANES), jnp.float32) for _ in range(modes))
+        hidden = lax.fori_loop(part * mid, (part + 1) * mid, step, start, unroll=4)
+        if not part:
+            for n in range(modes):
+                carried[n * SUB : (n + 1) * SUB, :] = hidden[n]
+
+    local_rows(0)
     state[...] = jnp.zeros_like(state)
     for step in range(1, stages):
         @pl.when(stage >= step)
@@ -408,6 +416,7 @@
         partial_sum(i)
         chunk_copy(i, first_target(i)).start()
 
+    local_rows(1)
     add_state(core, state, 1)
     add_state(1 - core, peer_state, 1)
     gate_rows(1)
@@ -488,6 +497,7 @@
             pltpu.VMEM(whole, f32),
             pltpu.VMEM(whole, f32),
             pltpu.VMEM(whole, f32),
+            pltpu.VMEM(whole, f32),
             pltpu.VMEM(half, f32),
             pltpu.VMEM(half, f32),
             pltpu.VMEM(half, f32),

time: 48.2 us -> 48.1 us (level)
  no operation moved by 1% of the time
where the time goes in v4:
time: 48.1 us; the launch traced here: 48 us
  Pallas kernels  47.2 us (98%)
  local copies, waits for them, and re-layouts  0.8 us (2%)
    pallas_call x1, Pallas kernels, fused(): pl.pallas_call(functools.partial(kernel, stages), out_shape=pltpu.VMEM((r...  47.2 us

profile of v4, /device:TPU:27, one launch (start us, length us, event | category | flops | bytes accessed | tf_op | source)
XLA Modules:
  0.0 48.0 jit_solution(12456054779993977435)
XLA Ops:
  0.0 47.2 %shard_map.64 = bf16[256,1024]{1,0:T(8,128)(2,1)S(1)} custom-call(bf16[256,1024]{1,0:T(8,128)(2,1)} %gate_hbm.1, bf16[256,1024]{1,0:T(8,128)(2,1)} %key_hbm.1, bf16[256,1024]{1,0:T(8,128)(2,1)} %value_hbm.1, f32[16,1024]{1,0:T(8,128)} %res_hbm.1, f32[16,1024]{1,0:T(8,128)} %decay_hbm.1, bf16[1024,4096]{1,0:T(8,128)(2,1)} %w_hbm.1), custom_call_target="tpu_custom_call" | custom-call | flops 2147483648 | bytes 8388608 | tf_op jit(solution)/shard_map/pallas_call | solution.py:480
  47.2 0.8 %copy.8 = bf16[256,1024]{1,0:T(8,128)(2,1)} copy(bf16[256,1024]{1,0:T(8,128)(2,1)S(1)} %shard_map.64) | data formatting | bytes 1048576

commit v5 on v4

--- a/solution.py
+++ b/solution.py
@@ -163,10 +163,11 @@
 MESH = pl.DeviceIdType.MESH
 LANES = 128
 SUB = 8
-WIDE = 512
-CHUNKS = 16
-FORWARDS = 4
+WIDE = 256
+CHUNKS = 32
+FORWARDS = 8
 SLABS = 4
+PIECES = 2
 
 
 def tree_sum(terms):
@@ -222,8 +223,8 @@
         load.start()
 
     def w_copy(i):
-        owner = (across, along_y if i % 2 else along_x, along_x if i % 2 else along_y, chan)[i // 2]
-        column = owner * (2 * WIDE) + (i % 2) * WIDE
+        owner = (across, along_y if i % 2 else along_x, along_x if i % 2 else along_y, chan)[i // 4]
+        column = owner * (4 * WIDE) + (i % 2) * 2 * WIDE + (i // 2 % 2) * WIDE
         return pltpu.make_async_copy(
             w_hbm.at[:, pl.ds(pl.multiple_of(column, WIDE), WIDE)], wbuf.at[i], w_sem.at[i]
         )
@@ -267,50 +268,62 @@
 
     mid = rows // 2
 
-    def end_states(half, dst):
-        lams = [lam[mode_rows(half, n), :] for n in range(half_modes)]
+    quarter = rows // 4
+    piece_modes = half_modes // PIECES
+    piece_size = piece_modes * SUB
+
+    def end_states(half, piece, dst):
+        numbers = range(piece * piece_modes, (piece + 1) * piece_modes)
+        lams = [lam[mode_rows(half, n), :] for n in numbers]
 
         def step(t, carry):
-            low, high = carry
-            x_low = xs[vec(t), :]
-            x_high = xs[vec(t + mid), :]
-            low = tuple(l * h + x_low for l, h in zip(lams, low))
-            high = tuple(l * h + x_high for l, h in zip(lams, high))
-            return (low, high)
-
-        zero = tuple(jnp.zeros((SUB, LANES), jnp.float32) for _ in range(half_modes))
-        low, high = lax.fori_loop(0, mid, step, (zero, zero), unroll=4)
-        for n in range(half_modes):
-            shrink = jnp.exp(dec[mode_rows(half, n), :] * float(-mid))
-            dst[n * SUB : (n + 1) * SUB, :] = shrink * low[n] + high[n]
-
-    end_states(1 - core, give)
-    pl.semaphore_wait(barrier, 3 + stages - 1)
-    send_end = pltpu.make_async_remote_copy(
-        src_ref=give, dst_ref=peer_end, send_sem=pair_send.at[0], recv_sem=pair_recv.at[0],
-        device_id=(chan, partner), device_id_type=MESH,
-    )
-    send_end.start()
-    end_states(core, ends)
-    send_end.wait_recv()
-
-    own_decay = dec[half_rows(core), :]
-    span = jnp.exp(own_decay * float(-rows))
-    is_first = core == 0
-    end_first = jnp.where(is_first, ends[...], peer_end[...])
-    end_second = jnp.where(is_first, peer_end[...], ends[...])
-    chip[...] = span * end_first + end_second
-
-    def push(step):
+            now = [xs[vec(t + q * quarter), :] for q in range(4)]
+            return tuple(tuple(l * h + x for l, h in zip(lams, hidden)) for x, hidden in zip(now, carry))
+
+        zero = tuple(jnp.zeros((SUB, LANES), jnp.float32) for _ in numbers)
+        parts = lax.fori_loop(0, quarter, step, (zero,) * 4, unroll=4)
+        for k, n in enumerate(numbers):
+            shrink = jnp.exp(dec[mode_rows(half, n), :] * float(-quarter))
+            total = parts[0][k]
+            for q in range(1, 4):
+                total = shrink * total + parts[q][k]
+            dst[n * SUB : (n + 1) * SUB, :] = total
+
+    def send_end(piece):
+        here = pl.ds(piece * piece_size, piece_size)
         return pltpu.make_async_remote_copy(
-            src_ref=chip, dst_ref=zbuf.at[step - 1], send_sem=z_send.at[step - 1], recv_sem=z_recv.at[step - 1],
+            src_ref=give.at[here, :], dst_ref=peer_end.at[here, :],
+            send_sem=pair_send.at[piece], recv_sem=pair_recv.at[piece],
+            device_id=(chan, partner), device_id_type=MESH,
+        )
+
+    def push(step, piece):
+        here = pl.ds(piece * piece_size, piece_size)
+        sem = (step - 1) * PIECES + piece
+        return pltpu.make_async_remote_copy(
+            src_ref=chip.at[here, :], dst_ref=zbuf.at[step - 1, here, :],
+            send_sem=z_send.at[sem], recv_sem=z_recv.at[sem],
             device_id=(chan, lax.rem(stage + step, stages) * 2 + core), device_id_type=MESH,
         )
 
-    for step in range(1, stages):
-        @pl.when(stage + step < stages)
-        def _():
-            push(step).start()
+    is_first = core == 0
+    for piece in range(PIECES):
+        end_states(1 - core, piece, give)
+        if piece == 0:
+            pl.semaphore_wait(barrier, 3 + stages - 1)
+        send_end(piece).start()
+
+    for piece in range(PIECES):
+        end_states(core, piece, ends)
+        send_end(piece).wait_recv()
+        here = slice(piece * piece_size, (piece + 1) * piece_size)
+        rates = dec[pl.ds(pl.multiple_of(core * half_size + piece * piece_size, piece_size), piece_size), :]
+        own, peer = ends[here, :], peer_end[here, :]
+        chip[here, :] = jnp.exp(rates * float(-rows)) * jnp.where(is_first, own, peer) + jnp.where(is_first, peer, own)
+        for step in range(1, stages):
+            @pl.when(stage + step < stages)
+            def _():
+                push(step, piece).start()
 
     def local_rows(part):
         lams = [lam[n * SUB : (n + 1) * SUB, :] for n in range(modes)]
@@ -336,21 +349,22 @@
     for step in range(1, stages):
         @pl.when(stage >= step)
         def _():
-            push(step).wait_recv()
+            for piece in range(PIECES):
+                push(step, piece).wait_recv()
             weight = jnp.exp(dec[half_rows(core), :] * float(-2 * rows * (step - 1)))
             state[...] += weight * zbuf[step - 1]
 
+    span = jnp.exp(dec[half_rows(core), :] * float(-rows))
+    end_first = jnp.where(is_first, ends[...], peer_end[...])
     begin_first = state[...]
     begin_second = span * begin_first + end_first
     give_state[...] = jnp.where(is_first, begin_second, begin_first)
     send_state = pltpu.make_async_remote_copy(
-        src_ref=give_state, dst_ref=peer_state, send_sem=pair_send.at[1], recv_sem=pair_recv.at[1],
+        src_ref=give_state, dst_ref=peer_state, send_sem=pair_send.at[PIECES], recv_sem=pair_recv.at[PIECES],
         device_id=(chan, partner), device_id_type=MESH,
     )
     send_state.start()
     state[...] = jnp.where(is_first, begin_first, begin_second)
-
-    quarter = rows // 4
 
     def add_state(half, src, part):
         lams = [lam[mode_rows(half, n), :] for n in range(half_modes)]
@@ -397,10 +411,10 @@
         pltpu.make_async_copy(w_hbm.at[:, pl.ds(0, WIDE)], wbuf.at[i], w_sem.at[i]).wait()
 
     def block_of(i):
-        return i // 4 * 2 + lax.rem(i, 2)
+        return i // 8 * 4 + lax.rem(i, 4)
 
     def partial_sum(i):
-        part = lax.rem(i // 2, 2)
+        part = lax.rem(i // 4, 2)
         here = pl.ds(pl.multiple_of(part * mid, mid), mid)
         sbuf[i] = jnp.dot(gated[here, :], wbuf[block_of(i)], preferred_element_type=jnp.float32)
 
@@ -410,7 +424,7 @@
     loads[2].wait()
     gate_rows(0)
 
-    @pl.loop(0, 2)
+    @pl.loop(0, 4)
     def _(i):
         w_wait(i)
         partial_sum(i)
@@ -421,9 +435,9 @@
     add_state(1 - core, peer_state, 1)
     gate_rows(1)
 
-    @pl.loop(2, CHUNKS)
+    @pl.loop(4, CHUNKS)
     def _(i):
-        @pl.when(lax.rem(i // 2, 2) == 0)
+        @pl.when(lax.rem(i // 4, 2) == 0)
         def _():
             w_wait(block_of(i))
 
@@ -452,16 +466,19 @@
     @pl.loop(0, FORWARDS)
     def _(j):
         chunk_copy(j + 2 * FORWARDS, second_target(j)).wait_recv()
-        here = pl.ds(pl.multiple_of(j // 2 * mid, mid), mid)
-        cols = pl.ds(pl.multiple_of(lax.rem(j, 2) * WIDE, WIDE), WIDE)
+        here = pl.ds(pl.multiple_of(j // 4 * mid, mid), mid)
+        column = lax.rem(j, 2) * (2 * WIDE) + lax.rem(j // 2, 2) * WIDE
+        cols = pl.ds(pl.multiple_of(column, WIDE), WIDE)
         out[here, cols] = (sbuf[j + 3 * FORWARDS] + rbuf[j + 2 * FORWARDS]).astype(jnp.bfloat16)
 
-    send_end.wait_send()
+    for piece in range(PIECES):
+        send_end(piece).wait_send()
     send_state.wait_send()
     for step in range(1, stages):
         @pl.when(stage + step < stages)
         def _():
-            push(step).wait_send()
+            for piece in range(PIECES):
+                push(step, piece).wait_send()
 
     @pl.loop(0, FORWARDS)
     def _(j):
@@ -479,7 +496,7 @@
     dma = pltpu.SemaphoreType.DMA
     return pl.pallas_call(
         functools.partial(kernel, stages),
-        out_shape=pltpu.VMEM((rows, 2 * WIDE), bf16),
+        out_shape=pltpu.VMEM((rows, 4 * WIDE), bf16),
         in_specs=[pl.BlockSpec(memory_space=pltpu.HBM)] * 6,
         out_specs=pl.BlockSpec(memory_space=pltpu.VMEM),
         scratch_shapes=[
@@ -510,23 +527,23 @@
             dma((CHUNKS // 2,)),
             dma((3 * FORWARDS,)),
             dma((3 * FORWARDS,)),
-            dma((2,)),
-            dma((2,)),
-            dma((stages - 1,)),
-            dma((stages - 1,)),
+            dma((PIECES + 1,)),
+            dma((PIECES + 1,)),
+            dma((PIECES * (stages - 1),)),
+            dma((PIECES * (stages - 1),)),
         ],
         compiler_params=pltpu.CompilerParams(
             collective_id=0, has_side_effects=True, vmem_limit_bytes=63 * 1024 * 1024
         ),
         cost_estimate=pl.CostEstimate(
-            flops=2 * rows * channels * 8 * WIDE, bytes_accessed=2 * channels * 8 * WIDE, transcendentals=0
+            flops=2 * rows * channels * 16 * WIDE, bytes_accessed=2 * channels * 16 * WIDE, transcendentals=0
         ),
     )(gate_stream, key_stream, value_stream, residues, decay_rates, out_weight)
 
 
 def run(*arrays):
     square = lax.axis_size("chan") == 4 and lax.axis_size("ctx") % 2 == 0 and lax.axis_size("ctx") > 2
-    fits = arrays[0].shape[1] == SUB * LANES and arrays[5].shape[1] == 8 * WIDE
+    fits = arrays[0].shape[1] == SUB * LANES and arrays[5].shape[1] == 16 * WIDE
     return (fused if square and fits else on_device)(*arrays)
 
 

time: 48.1 us -> 48.1 us (level)
  no operation moved by 1% of the time
where the time goes in v5:
time: 48.1 us; the launch traced here: 48 us
  Pallas kernels  47.2 us (98%)
  local copies, waits for them, and re-layouts  0.8 us (2%)
    pallas_call x1, Pallas kernels, fused(): pl.pallas_call(functools.partial(kernel, stages), out_shape=pltpu.VMEM((r...  47.2 us

profile of v5, /device:TPU:27, one launch (start us, length us, event | category | flops | bytes accessed | tf_op | source)
XLA Modules:
  0.0 48.0 jit_solution(3538968042917035669)
XLA Ops:
  0.0 47.2 %shard_map.64 = bf16[256,1024]{1,0:T(8,128)(2,1)S(1)} custom-call(bf16[256,1024]{1,0:T(8,128)(2,1)} %gate_hbm.1, bf16[256,1024]{1,0:T(8,128)(2,1)} %key_hbm.1, bf16[256,1024]{1,0:T(8,128)(2,1)} %value_hbm.1, f32[16,1024]{1,0:T(8,128)} %res_hbm.1, f32[16,1024]{1,0:T(8,128)} %decay_hbm.1, bf16[1024,4096]{1,0:T(8,128)(2,1)} %w_hbm.1), custom_call_target="tpu_custom_call" | custom-call | flops 2147483648 | bytes 8388608 | tf_op jit(solution)/shard_map/pallas_call | solution.py:497
  47.2 0.8 %copy.8 = bf16[256,1024]{1,0:T(8,128)(2,1)} copy(bf16[256,1024]{1,0:T(8,128)(2,1)S(1)} %shard_map.64) | data formatting | bytes 1048576

commit v6 on v4

--- a/solution.py
+++ b/solution.py
@@ -399,10 +399,22 @@
     def block_of(i):
         return i // 4 * 2 + lax.rem(i, 2)
 
+    def slot_of(i):
+        paired = i // 4 * 4 + lax.rem(i, 2) * 2 + lax.rem(i // 2, 2)
+        return jnp.where(i // 4 == 1, paired, i)
+
+    def direct_copy(parity):
+        both = pl.ds(FORWARDS + 2 * parity, 2)
+        return pltpu.make_async_remote_copy(
+            src_ref=sbuf.at[both], dst_ref=rbuf.at[both],
+            send_sem=chunk_send.at[FORWARDS + parity], recv_sem=chunk_recv.at[FORWARDS + parity],
+            device_id=(first_target(parity), ctx), device_id_type=MESH,
+        )
+
     def partial_sum(i):
         part = lax.rem(i // 2, 2)
         here = pl.ds(pl.multiple_of(part * mid, mid), mid)
-        sbuf[i] = jnp.dot(gated[here, :], wbuf[block_of(i)], preferred_element_type=jnp.float32)
+        sbuf[slot_of(i)] = jnp.dot(gated[here, :], wbuf[block_of(i)], preferred_element_type=jnp.float32)
 
     add_state(core, state, 0)
     send_state.wait_recv()
@@ -433,10 +445,9 @@
         def _():
             chunk_copy(i, first_target(i)).start()
 
-    @pl.loop(0, FORWARDS)
-    def _(j):
-        chunk_copy(j, first_target(j)).wait_send()
-        chunk_copy(j + FORWARDS, first_target(j)).start()
+        @pl.when(i // 2 == 3)
+        def _():
+            direct_copy(lax.rem(i, 2)).start()
 
     @pl.loop(0, FORWARDS)
     def _(j):
@@ -444,10 +455,11 @@
         sbuf[j + 2 * FORWARDS] += rbuf[j]
         chunk_copy(j + 2 * FORWARDS, second_target(j)).start()
 
-    @pl.loop(0, FORWARDS)
-    def _(j):
-        chunk_copy(j + FORWARDS, first_target(j)).wait_recv()
-        sbuf[j + 3 * FORWARDS] += rbuf[j + FORWARDS]
+    @pl.loop(0, 2)
+    def _(parity):
+        direct_copy(parity).wait_recv()
+        for k in range(2):
+            sbuf[3 * FORWARDS + 2 * k + parity] += rbuf[FORWARDS + 2 * parity + k]
 
     @pl.loop(0, FORWARDS)
     def _(j):
@@ -458,6 +470,8 @@
 
     send_end.wait_send()
     send_state.wait_send()
+    for parity in range(2):
+        direct_copy(parity).wait_send()
     for step in range(1, stages):
         @pl.when(stage + step < stages)
         def _():
@@ -465,7 +479,7 @@
 
     @pl.loop(0, FORWARDS)
     def _(j):
-        chunk_copy(j + FORWARDS, first_target(j)).wait_send()
+        chunk_copy(j, first_target(j)).wait_send()
         chunk_copy(j + 2 * FORWARDS, second_target(j)).wait_send()
 
 

time: 48.1 us -> 48.1 us (level)
  no operation moved by 1% of the time
where the time goes in v6:
time: 48.1 us; the launch traced here: 48 us
  Pallas kernels  47.2 us (98%)
  local copies, waits for them, and re-layouts  0.8 us (2%)
    pallas_call x1, Pallas kernels, fused(): pl.pallas_call(functools.partial(kernel, stages), out_shape=pltpu.VMEM((r...  47.2 us

profile of v6, /device:TPU:27, one launch (start us, length us, event | category | flops | bytes accessed | tf_op | source)
XLA Modules:
  0.0 48.0 jit_solution(6930473031576528587)
XLA Ops:
  0.0 47.2 %shard_map.64 = bf16[256,1024]{1,0:T(8,128)(2,1)S(1)} custom-call(bf16[256,1024]{1,0:T(8,128)(2,1)} %gate_hbm.1, bf16[256,1024]{1,0:T(8,128)(2,1)} %key_hbm.1, bf16[256,1024]{1,0:T(8,128)(2,1)} %value_hbm.1, f32[16,1024]{1,0:T(8,128)} %res_hbm.1, f32[16,1024]{1,0:T(8,128)} %decay_hbm.1, bf16[1024,4096]{1,0:T(8,128)(2,1)} %w_hbm.1), custom_call_target="tpu_custom_call" | custom-call | flops 2147483648 | bytes 8388608 | tf_op jit(solution)/shard_map/pallas_call | solution.py:494
  47.2 0.8 %copy.8 = bf16[256,1024]{1,0:T(8,128)(2,1)} copy(bf16[256,1024]{1,0:T(8,128)(2,1)S(1)} %shard_map.64) | data formatting | bytes 1048576

commit v7 on v5

--- a/solution.py
+++ b/solution.py
@@ -163,9 +163,9 @@
 MESH = pl.DeviceIdType.MESH
 LANES = 128
 SUB = 8
-WIDE = 256
-CHUNKS = 32
-FORWARDS = 8
+WIDE = 512
+CHUNKS = 16
+FORWARDS = 4
 SLABS = 4
 PIECES = 2
 
@@ -223,8 +223,8 @@
         load.start()
 
     def w_copy(i):
-        owner = (across, along_y if i % 2 else along_x, along_x if i % 2 else along_y, chan)[i // 4]
-        column = owner * (4 * WIDE) + (i % 2) * 2 * WIDE + (i // 2 % 2) * WIDE
+        owner = (across, along_y if i % 2 else along_x, along_x if i % 2 else along_y, chan)[i // 2]
+        column = owner * (2 * WIDE) + (i % 2) * WIDE
         return pltpu.make_async_copy(
             w_hbm.at[:, pl.ds(pl.multiple_of(column, WIDE), WIDE)], wbuf.at[i], w_sem.at[i]
         )
@@ -411,12 +411,24 @@
         pltpu.make_async_copy(w_hbm.at[:, pl.ds(0, WIDE)], wbuf.at[i], w_sem.at[i]).wait()
 
     def block_of(i):
-        return i // 8 * 4 + lax.rem(i, 4)
+        return i // 4 * 2 + lax.rem(i, 2)
+
+    def slot_of(i):
+        paired = i // 4 * 4 + lax.rem(i, 2) * 2 + lax.rem(i // 2, 2)
+        return jnp.where(i // 4 == 1, paired, i)
+
+    def direct_copy(parity):
+        both = pl.ds(FORWARDS + 2 * parity, 2)
+        return pltpu.make_async_remote_copy(
+            src_ref=sbuf.at[both], dst_ref=rbuf.at[both],
+            send_sem=chunk_send.at[FORWARDS + parity], recv_sem=chunk_recv.at[FORWARDS + parity],
+            device_id=(first_target(parity), ctx), device_id_type=MESH,
+        )
 
     def partial_sum(i):
-        part = lax.rem(i // 4, 2)
+        part = lax.rem(i // 2, 2)
         here = pl.ds(pl.multiple_of(part * mid, mid), mid)
-        sbuf[i] = jnp.dot(gated[here, :], wbuf[block_of(i)], preferred_element_type=jnp.float32)
+        sbuf[slot_of(i)] = jnp.dot(gated[here, :], wbuf[block_of(i)], preferred_element_type=jnp.float32)
 
     add_state(core, state, 0)
     send_state.wait_recv()
@@ -424,7 +436,7 @@
     loads[2].wait()
     gate_rows(0)
 
-    @pl.loop(0, 4)
+    @pl.loop(0, 2)
     def _(i):
         w_wait(i)
         partial_sum(i)
@@ -435,9 +447,9 @@
     add_state(1 - core, peer_state, 1)
     gate_rows(1)
 
-    @pl.loop(4, CHUNKS)
+    @pl.loop(2, CHUNKS)
     def _(i):
-        @pl.when(lax.rem(i // 4, 2) == 0)
+        @pl.when(lax.rem(i // 2, 2) == 0)
         def _():
             w_wait(block_of(i))
 
@@ -447,10 +459,9 @@
         def _():
             chunk_copy(i, first_target(i)).start()
 
-    @pl.loop(0, FORWARDS)
-    def _(j):
-        chunk_copy(j, first_target(j)).wait_send()
-        chunk_copy(j + FORWARDS, first_target(j)).start()
+        @pl.when(i // 2 == 3)
+        def _():
+            direct_copy(lax.rem(i, 2)).start()
 
     @pl.loop(0, FORWARDS)
     def _(j):
@@ -458,22 +469,24 @@
         sbuf[j + 2 * FORWARDS] += rbuf[j]
         chunk_copy(j + 2 * FORWARDS, second_target(j)).start()
 
-    @pl.loop(0, FORWARDS)
-    def _(j):
-        chunk_copy(j + FORWARDS, first_target(j)).wait_recv()
-        sbuf[j + 3 * FORWARDS] += rbuf[j + FORWARDS]
+    @pl.loop(0, 2)
+    def _(parity):
+        direct_copy(parity).wait_recv()
+        for k in range(2):
+            sbuf[3 * FORWARDS + 2 * k + parity] += rbuf[FORWARDS + 2 * parity + k]
 
     @pl.loop(0, FORWARDS)
     def _(j):
         chunk_copy(j + 2 * FORWARDS, second_target(j)).wait_recv()
-        here = pl.ds(pl.multiple_of(j // 4 * mid, mid), mid)
-        column = lax.rem(j, 2) * (2 * WIDE) + lax.rem(j // 2, 2) * WIDE
-        cols = pl.ds(pl.multiple_of(column, WIDE), WIDE)
+        here = pl.ds(pl.multiple_of(j // 2 * mid, mid), mid)
+        cols = pl.ds(pl.multiple_of(lax.rem(j, 2) * WIDE, WIDE), WIDE)
         out[here, cols] = (sbuf[j + 3 * FORWARDS] + rbuf[j + 2 * FORWARDS]).astype(jnp.bfloat16)
 
     for piece in range(PIECES):
         send_end(piece).wait_send()
     send_state.wait_send()
+    for parity in range(2):
+        direct_copy(parity).wait_send()
     for step in range(1, stages):
         @pl.when(stage + step < stages)
         def _():
@@ -482,7 +495,7 @@
 
     @pl.loop(0, FORWARDS)
     def _(j):
-        chunk_copy(j + FORWARDS, first_target(j)).wait_send()
+        chunk_copy(j, first_target(j)).wait_send()
         chunk_copy(j + 2 * FORWARDS, second_target(j)).wait_send()
 
 
@@ -496,7 +509,7 @@
     dma = pltpu.SemaphoreType.DMA
     return pl.pallas_call(
         functools.partial(kernel, stages),
-        out_shape=pltpu.VMEM((rows, 4 * WIDE), bf16),
+        out_shape=pltpu.VMEM((rows, 2 * WIDE), bf16),
         in_specs=[pl.BlockSpec(memory_space=pltpu.HBM)] * 6,
         out_specs=pl.BlockSpec(memory_space=pltpu.VMEM),
         scratch_shapes=[
@@ -536,14 +549,14 @@
             collective_id=0, has_side_effects=True, vmem_limit_bytes=63 * 1024 * 1024
         ),
         cost_estimate=pl.CostEstimate(
-            flops=2 * rows * channels * 16 * WIDE, bytes_accessed=2 * channels * 16 * WIDE, transcendentals=0
+            flops=2 * rows * channels * 8 * WIDE, bytes_accessed=2 * channels * 8 * WIDE, transcendentals=0
         ),
     )(gate_stream, key_stream, value_stream, residues, decay_rates, out_weight)
 
 
 def run(*arrays):
     square = lax.axis_size("chan") == 4 and lax.axis_size("ctx") % 2 == 0 and lax.axis_size("ctx") > 2
-    fits = arrays[0].shape[1] == SUB * LANES and arrays[5].shape[1] == 16 * WIDE
+    fits = arrays[0].shape[1] == SUB * LANES and arrays[5].shape[1] == 8 * WIDE
     return (fused if square and fits else on_device)(*arrays)
 
 

time: 48.1 us -> 48 us (level)
  no operation moved by 1% of the time
where the time goes in v7:
time: 48 us; the launch traced here: 47.8 us
  Pallas kernels  47 us (98%)
  local copies, waits for them, and re-layouts  0.8 us (2%)
    pallas_call x1, Pallas kernels, fused(): pl.pallas_call(functools.partial(kernel, stages), out_shape=pltpu.VMEM((r...  47 us

profile of v7, /device:TPU:27, one launch (start us, length us, event | category | flops | bytes accessed | tf_op | source)
XLA Modules:
  0.0 47.8 jit_solution(12623591885785433710)
XLA Ops:
  0.0 47.0 %shard_map.64 = bf16[256,1024]{1,0:T(8,128)(2,1)S(1)} custom-call(bf16[256,1024]{1,0:T(8,128)(2,1)} %gate_hbm.1, bf16[256,1024]{1,0:T(8,128)(2,1)} %key_hbm.1, bf16[256,1024]{1,0:T(8,128)(2,1)} %value_hbm.1, f32[16,1024]{1,0:T(8,128)} %res_hbm.1, f32[16,1024]{1,0:T(8,128)} %decay_hbm.1, bf16[1024,4096]{1,0:T(8,128)(2,1)} %w_hbm.1), custom_call_target="tpu_custom_call" | custom-call | flops 2147483648 | bytes 8388608 | tf_op jit(solution)/shard_map/pallas_call | solution.py:510
  47.0 0.8 %copy.8 = bf16[256,1024]{1,0:T(8,128)(2,1)} copy(bf16[256,1024]{1,0:T(8,128)(2,1)S(1)} %shard_map.64) | data formatting | bytes 1048576
